TPU v7x, 32 devices: a whole 2x2x4 slice. The times are simulated.
32 devices in a mesh: groups: 2 (over y), space: 8 (over z, x), heads: 2 (over core).
Axes of the slice: x: 2, y: 2, z: 4, core: 2. Of those that a mesh axis runs over, the one named last changes fastest.
Arguments:
- queries: bfloat16 [2400, 1536], P(('groups', 'space'), 'heads'), parts along dimension 0, may hold values from -16 to 16
- latent_keys: bfloat16 [2400, 1536], P(('groups', 'space'), 'heads'), parts along dimension 0, may hold values from -9 to 9
- latent_values: bfloat16 [2400, 1536], P(('groups', 'space'), 'heads'), parts along dimension 0, may hold values from -6 to 6
- prompt: bfloat16 [512, 3072], P('groups'), parts along dimension 0, may hold values from -44 to 44
- key_weight: bfloat16 [3072, 1536], P('space', 'heads'), may hold values from -0.15625 to 0.15625
- value_weight: bfloat16 [3072, 1536], P('space', 'heads'), may hold values from -0.15625 to 0.15625
- out_weight: bfloat16 [1536, 3072], P('heads', 'space'), may hold values from -0.21875 to 0.21875
- tile_owner: int32 [16], P('groups'), parts along dimension 0, may hold values from 0 to 7, as said below
Outputs:
- block_output: bfloat16 [2400, 3072], P(('groups', 'space'), 'heads'), parts along dimension 0
There are 2 independent parts, one for each index of `groups`. A program takes and returns all parts, laid end to end along the dimension named above; an argument that names none is the same for every part. Nothing has to cross between parts.
Inputs may be any that keep to these rules, and one draw needn't show every extreme that they name: `tile_owner`: tile t = i * 2 + j of the 4 x 2 grid is held by slot a * 2 + b, with a = (i + r) mod 4 or a = (3 - i + r) mod 4 for one r, and b = j or b = 1 - j; r and each of the two alternatives are the same for all tiles.
All inputs are finite; a program needn't handle non-finite values.
Results may differ from a plain program's by a relative error of at most 0.0081.
Values may be sent and summed in bfloat16 or wider, within the bound.
A program may use at most 64 MiB of HBM per device.

v0:
```python
import jax
import jax.numpy as jnp
from jax import lax
from jax.sharding import PartitionSpec as P

HD = 128
RT = 16
RH = 56
TILE = 5
rope_theta = 256.0
eps_norm = 1e-06
masked_score = -1e30


def shifted(value, axis, steps):
    count = lax.axis_size(axis)
    pairs = [(source, (source + steps) % count) for source in range(count)]
    return lax.ppermute(value, axis, pairs)


def rope_tables(frame_pos, height_pos, width_pos):
    pairs_time = jnp.arange(RT // 2, dtype=jnp.float32)
    pairs_space = jnp.arange(RH // 2, dtype=jnp.float32)
    freq_time = rope_theta ** (-2.0 * pairs_time / RT)
    freq_space = rope_theta ** (-2.0 * pairs_space / RH)
    angles = jnp.concatenate(
        [
            frame_pos[:, None] * freq_time[None, :],
            height_pos[:, None] * freq_space[None, :],
            width_pos[:, None] * freq_space[None, :],
        ],
        axis=1,
    )
    return (jnp.cos(angles), jnp.sin(angles))


def rotate(stacked, cosine, sine_table):
    row_count = stacked.shape[0]
    head_total = stacked.shape[1]
    paired = stacked.reshape(row_count, head_total, HD // 2, 2)
    even_part = paired[..., 0]
    odd_part = paired[..., 1]
    cos_rows = cosine[:, None, :]
    sin_rows = sine_table[:, None, :]
    turned = jnp.stack(
        [even_part * cos_rows - odd_part * sin_rows, even_part * sin_rows + odd_part * cos_rows],
        axis=-1,
    )
    return turned.reshape(row_count, head_total * HD)


def normalize_keys(summed, head_total):
    row_count = summed.shape[0]
    half_width = summed.shape[1] // 2
    key_part = summed[:, :half_width].reshape(row_count, head_total, HD)
    key_part = key_part * lax.rsqrt(
        jnp.mean(key_part * key_part, axis=-1, keepdims=True) + eps_norm
    )
    return jnp.concatenate(
        [key_part.reshape(row_count, half_width), summed[:, half_width:]], axis=1
    ).astype(jnp.bfloat16)


def body(
    queries, latent_keys, latent_values, prompt, key_weight, value_weight, out_weight, tile_owner
):
    spaces = lax.axis_size("space")
    device = lax.axis_index("space")
    grid_h = min(8, spaces // 2)
    grid_w = spaces // grid_h
    tok_rows = queries.shape[0]
    head_width = queries.shape[1]
    head_count = head_width // HD
    tile_total = tile_owner.shape[0]
    tile_index = jnp.arange(tile_total, dtype=jnp.int32)
    own_tile = jnp.sum(jnp.where(tile_owner == device, tile_index, 0))
    tile_row = own_tile // grid_w
    tile_col = own_tile % grid_w
    anchor_slot = tile_owner[0]
    right_slot = tile_owner[min(1, tile_total - 1)]
    lower_slot = tile_owner[min(grid_w, tile_total - 1)]
    col_sign = jnp.where(right_slot % grid_w - anchor_slot % grid_w == -1, -1, 1)
    row_sign = jnp.where((lower_slot // grid_w - anchor_slot // grid_w) % grid_h == 1, 1, -1)
    cell_index = jnp.arange(tok_rows, dtype=jnp.int32)
    frame_pos = (cell_index // (TILE * TILE)).astype(jnp.float32)
    height_pos = (tile_row * TILE + cell_index // TILE % TILE).astype(jnp.float32)
    width_pos = (tile_col * TILE + cell_index % TILE).astype(jnp.float32)
    cosine, sine_table = rope_tables(frame_pos, height_pos, width_pos)
    query_rot = rotate(
        queries.astype(jnp.float32).reshape(tok_rows, head_count, HD), cosine, sine_table
    ).astype(jnp.bfloat16)
    key_rot = rotate(
        latent_keys.astype(jnp.float32).reshape(tok_rows, head_count, HD), cosine, sine_table
    ).astype(jnp.bfloat16)
    width_rows = key_weight.shape[0]
    text_cols = lax.dynamic_slice_in_dim(prompt, device * width_rows, width_rows, 1)
    both_weights = jnp.concatenate([key_weight, value_weight], axis=1)
    partial_text = jnp.dot(text_cols, both_weights, preferred_element_type=jnp.float32)
    summed_text = lax.psum(partial_text, "space")
    text_kv = normalize_keys(summed_text, head_count)
    kv_own = jnp.concatenate([key_rot, latent_values], axis=1)
    blocks = []
    valid_parts = []
    for row_step in (-1, 0, 1):
        for col_step in (-1, 0, 1):
            if row_step == 0 and col_step == 0:
                fetched = kv_own
            else:
                fetched = shifted(kv_own, "space", -(row_step * grid_w + col_step))
            near_row = tile_row + row_sign * row_step
            near_col = tile_col + col_sign * col_step
            inside = (near_row >= 0) & (near_row < grid_h) & (near_col >= 0) & (near_col < grid_w)
            blocks.append(fetched)
            valid_parts.append(jnp.zeros((tok_rows,), jnp.int32) + inside.astype(jnp.int32))
    blocks.append(text_kv)
    valid_parts.append(jnp.ones((text_kv.shape[0],), jnp.int32))
    keys_all = jnp.concatenate(blocks, axis=0)
    key_valid = jnp.concatenate(valid_parts, axis=0)
    score_scale = HD ** (-0.5)
    head_outputs = []
    for head_index in range(head_count):
        head_start = head_index * HD
        query_slice = query_rot[:, head_start : head_start + HD]
        key_slice = keys_all[:, head_start : head_start + HD]
        value_slice = keys_all[:, head_width + head_start : head_width + head_start + HD]
        scores = (
            lax.dot_general(
                query_slice, key_slice, (((1,), (1,)), ((), ())), preferred_element_type=jnp.float32
            )
            * score_scale
        )
        scores = jnp.where(key_valid[None, :] > 0, scores, masked_score)
        top_score = jnp.max(scores, axis=-1, keepdims=True)
        exponent = jnp.exp(scores - top_score)
        weights = (exponent / jnp.sum(exponent, axis=-1, keepdims=True)).astype(jnp.bfloat16)
        head_outputs.append(
            jnp.dot(weights, value_slice, preferred_element_type=jnp.float32).astype(jnp.bfloat16)
        )
    attended = jnp.concatenate(head_outputs, axis=1)
    partial_out = jnp.dot(
        attended,
        lax.all_gather(out_weight, "space", axis=1, tiled=True),
        preferred_element_type=jnp.float32,
    )
    summed_out = lax.psum_scatter(
        partial_out.astype(jnp.bfloat16), "heads", scatter_dimension=1, tiled=True
    )
    return summed_out


def solution(mesh):
    in_specs = (
        P(("groups", "space"), "heads"),
        P(("groups", "space"), "heads"),
        P(("groups", "space"), "heads"),
        P("groups", None),
        P("space", "heads"),
        P("space", "heads"),
        P("heads", "space"),
        P("groups"),
    )
    out_specs = P(("groups", "space"), "heads")
    return jax.shard_map(body, mesh=mesh, in_specs=in_specs, out_specs=out_specs, check_vma=False)
```

profile of v0, /device:TPU:0, one launch (start us, length us, event | category | flops | bytes accessed | tf_op | source)
XLA Modules:
  0.0 252.2 jit_solution(18399292161967376809)
XLA Ops:
  6.6 1.4 copy-done
  7.9 3.0 %fusion.6 = f32[256,1536]{1,0:T(8,128)} fusion(bf16[384,768]{1,0:T(8,128)(2,1)} %param.13, bf16[384,768]{1,0:T(8,128)(2,1)} %param.12, bf16[256,3072]{1,0:T(8,128)(2,1)S(1)} %copy-done, s32[]{:T(128)S(6)} %select_n.110), kind=kOutput, calls=%fused_computation.13 | convolution fusion | flops 304349184 | bytes 2949124 | tf_op jit(solution)/shard_map/dot_general | solution.py:98
  10.9 0.0 all-reduce.2.cloned.1.call-update
  10.9 0.0 all-gather.2.cloned.1.call-start
  11.0 0.7 all-gather.2.cloned.1.call-update
  11.7 0.0 reduce-scatter.2.cloned.1.call-start
  11.7 0.6 fusion.51
  15.0 0.2 copy.9
  15.2 0.5 reshape.201
  15.7 2.0 copy.10
  17.7 1.6 reshape.202
  19.3 0.1 broadcast_multiply_fusion.2
  19.4 0.1 broadcast_multiply_fusion.1
  19.5 0.2 fusion.42
  19.7 2.7 %subtract_convert_fusion.1 = (bf16[150,6,64,1]{0,3,2,1:T(2,128)(2,1)S(1)}, bf16[150,6,64,1]{0,3,2,1:T(2,128)(2,1)}, bf16[150,6,64,1]{0,3,2,1:T(2,128)(2,1)S(1)}, bf16[150,6,64,1]{0,3,2,1:T(2,128)(2,1)S(1)}) fusion(f32[150,6,64,2]{0,3,2,1:T(2,128)S(1)} %reshape.201, f32[150,64]{0,1:T(8,128)S(1)} %get-tuple-element.12, f32[150,64]{0,1:T(8,128)S(1)} %get-tuple-element.11, ...), kind=kLoop, calls=%fused_computation.69 | loop fusion | flops 921600 | bytes 1459200 | tf_op jit(solution)/shard_map/convert.7
  22.5 1.0 pad_maximum_fusion.3
  23.4 0.4 convert_element_type.111
  23.8 0.1 copy.11
  24.0 1.7 pad_maximum_fusion.1
  25.7 4.0 %collective-permute-start = (bf16[150,1536]{1,0:T(8,128)(2,1)}, bf16[150,1536]{1,0:T(8,128)(2,1)}, u32[]{:S(2)}, u32[]{:S(2)}) collective-permute-start(bf16[150,1536]{1,0:T(8,128)(2,1)} %pad_maximum_fusion.1), channel_id=1, source_target_pairs={{0,6},{2,8},{4,10},{6,12},{8,14},{10,0},{12,2},{14,4},{1,7},{3,9},... | collective-permute-start | bytes 1382408 | tf_op jit(solution)/shard_map/ppermute | solution.py:18
  29.7 1.6 collective-permute-start.1
  31.3 1.5 collective-permute-start.2
  32.8 3.2 %collective-permute-start.3 = (bf16[150,1536]{1,0:T(8,128)(2,1)}, bf16[150,1536]{1,0:T(8,128)(2,1)}, u32[]{:S(2)}, u32[]{:S(2)}) collective-permute-start(bf16[150,1536]{1,0:T(8,128)(2,1)} %pad_maximum_fusion.1), channel_id=1, source_target_pairs={{0,14},{2,0},{4,2},{6,4},{8,6},{10,8},{12,10},{14,12},{1,15},{3,1}... | collective-permute-start | bytes 1382408 | tf_op jit(solution)/shard_map/ppermute | solution.py:18
  36.0 0.5 collective-permute-start.4
  36.5 0.6 fusion.54
  43.3 2.0 pad_maximum_fusion.2
  45.3 1.1 convert_element_type.110
  46.5 0.1 concatenate.34
  46.6 91.5 %all-reduce.2.cloned.1.call-done = f32[256,1536]{1,0:T(8,128)} async-done(((f32[256,1536]{1,0:T(8,128)}), f32[256,1536]{1,0:T(8,128)}) %all-reduce.2.cloned.1.call-update) | async-done | bytes 1572880 | tf_op jit(solution)/shard_map/psum | solution.py:99
  138.1 1.2 slice_multiply_fusion
  139.3 0.3 copy.12
  139.6 0.1 reduce_sum.73
  139.6 0.1 mul.191
  139.7 0.3 copy.13
  140.0 1.2 slice.180
  141.1 0.0 collective-permute-done
  141.2 3.0 %collective-permute-start.5 = (bf16[150,1536]{1,0:T(8,128)(2,1)}, bf16[150,1536]{1,0:T(8,128)(2,1)S(1)}, u32[]{:S(2)}, u32[]{:S(2)}) collective-permute-start(bf16[150,1536]{1,0:T(8,128)(2,1)} %pad_maximum_fusion.1), channel_id=1, source_target_pairs={{0,10},{2,12},{4,14},{6,0},{8,2},{10,4},{12,6},{14,8},{1,11},{3,13... | collective-permute-start | bytes 1382408 | tf_op jit(solution)/shard_map/ppermute | solution.py:18
  144.1 1.2 multiply_convert_fusion
  145.3 0.1 pad_maximum_fusion
  145.4 0.0 collective-permute-done.1
  145.4 16.0 %collective-permute-done.5 = bf16[150,1536]{1,0:T(8,128)(2,1)S(1)} collective-permute-done((bf16[150,1536]{1,0:T(8,128)(2,1)}, bf16[150,1536]{1,0:T(8,128)(2,1)S(1)}, u32[]{:S(2)}, u32[]{:S(2)}) %collective-permute-start.5) | collective-permute-done | bytes 460832 | tf_op jit(solution)/shard_map/ppermute | solution.py:18
  161.5 34.4 %concatenate.39 = bf16[1606,1536]{1,0:T(8,128)(2,1)} concatenate(bf16[150,1536]{1,0:T(8,128)(2,1)} %collective-permute-done, bf16[150,1536]{1,0:T(8,128)(2,1)} %collective-permute-done.1, bf16[150,1536]{1,0:T(8,128)(2,1)} %collective-permute-done.2, bf16[150,1536]{1,0:T(8,128)(2,1)} %collective-permute-done.2, bf16[150,1536]{1,0:T(8,128)(2,1)} %pad_maximum_fusion.1, ...), dimensions={0} | concatenate | bytes 9867264 | tf_op jit(solution)/shard_map/concatenate | solution.py:117
  195.9 1.6 fusion.55
  197.5 0.3 fusion.16
  197.8 1.6 fusion.56
  199.4 0.3 fusion.17
  199.7 1.7 fusion.57
  201.4 0.3 fusion.18
  201.7 1.6 fusion.58
  203.3 0.3 fusion.19
  203.5 1.6 fusion.59
  205.1 0.3 fusion.20
  205.4 1.6 fusion.60
  207.0 0.3 fusion.21
  207.3 0.4 fusion.15
  207.7 0.4 fusion.14
  208.2 0.4 fusion.13
  208.6 0.4 fusion.12
  209.0 0.4 fusion.11
  209.4 0.4 fusion.10
  209.9 22.8 %all-gather.2.cloned.1.call-done = bf16[768,3072]{1,0:T(8,128)(2,1)} async-done(((bf16[768,384]{1,0:T(8,128)(2,1)}), bf16[768,3072]{1,0:T(8,128)(2,1)}) %all-gather.2.cloned.1.call-update) | async-done | bytes 4718608 | tf_op jit(solution)/shard_map/all_gather | solution.py:142
  232.6 4.2 %convolution_convert_fusion = bf16[150,3072]{1,0:T(8,128)(2,1)} fusion(bf16[150,768]{1,0:T(8,128)(2,1)S(1)} %fusion.10, bf16[768,3072]{1,0:T(8,128)(2,1)} %all-gather.2.cloned.1.call-done), kind=kOutput, calls=%fused_computation | convolution fusion | flops 708249600 | bytes 5870592 | tf_op jit(solution)/shard_map/dot_general | solution.py:140
  236.8 0.0 reduce-scatter.2.cloned.1.call-update
  236.8 8.8 %reduce-scatter.2.cloned.1.call-done = bf16[150,1536]{1,0:T(8,128)(2,1)} async-done(((bf16[150,3072]{1,0:T(8,128)(2,1)}), bf16[150,1536]{1,0:T(8,128)(2,1)}) %reduce-scatter.2.cloned.1.call-update) | async-done | bytes 460816 | tf_op jit(solution)/shard_map/reduce_scatter | solution.py:145
  (27 shorter events, 0.1 us)
Async XLA Ops:
  6.5 1.4 copy-start
  6.5 5.2 %copy-start.3 = (s32[8]{0:T(128)S(1)}, s32[8]{0:T(128)}, u32[]{:S(2)}) copy-start(s32[8]{0:T(128)} %param.15) | copy-start | bytes 100
  6.5 8.4 %copy-start.2 = (bf16[150,768]{1,0:T(8,128)(2,1)S(1)}, bf16[150,768]{1,0:T(8,128)(2,1)}, u32[]{:S(2)}) copy-start(bf16[150,768]{1,0:T(8,128)(2,1)} %param.8) | copy-start | bytes 691204
  6.5 131.5 %all-reduce.2.cloned.1.call-start = ((), (), s32[]{:S(2)}) async-start(), calls=%async_computation.1 | async-start | bytes 3145728 | tf_op jit(solution)/shard_map/psum | solution.py:99
  10.9 221.7 %all-gather.2.cloned.1.call-start = ((), (), s32[]{:S(2)}) async-start(), calls=%async_computation.2 | async-start | bytes 5308416 | tf_op jit(solution)/shard_map/all_gather | solution.py:142
  11.7 234.0 %reduce-scatter.2.cloned.1.call-start = ((), (), s32[]{:S(2)}) async-start(), calls=%async_computation.3 | async-start | bytes 1400832 | tf_op jit(solution)/shard_map/reduce_scatter | solution.py:145
  25.7 115.4 %collective-permute-start = (bf16[150,1536]{1,0:T(8,128)(2,1)}, bf16[150,1536]{1,0:T(8,128)(2,1)}, u32[]{:S(2)}, u32[]{:S(2)}) collective-permute-start(bf16[150,1536]{1,0:T(8,128)(2,1)} %pad_maximum_fusion.1), channel_id=1, source_target_pairs={{0,6},{2,8},{4,10},{6,12},{8,14},{10,0},{12,2},{14,4},{1,7},{3,9},... | collective-permute-start | bytes 1382408 | tf_op jit(solution)/shard_map/ppermute | solution.py:18
  29.7 115.7 %collective-permute-start.1 = (bf16[150,1536]{1,0:T(8,128)(2,1)}, bf16[150,1536]{1,0:T(8,128)(2,1)}, u32[]{:S(2)}, u32[]{:S(2)}) collective-permute-start(bf16[150,1536]{1,0:T(8,128)(2,1)} %pad_maximum_fusion.1), channel_id=1, source_target_pairs={{0,4},{2,6},{4,8},{6,10},{8,12},{10,14},{12,0},{14,2},{1,5},{3,7},... | collective-permute-start | bytes 1382408 | tf_op jit(solution)/shard_map/ppermute | solution.py:18
  31.3 114.1 %collective-permute-start.2 = (bf16[150,1536]{1,0:T(8,128)(2,1)}, bf16[150,1536]{1,0:T(8,128)(2,1)}, u32[]{:S(2)}, u32[]{:S(2)}) collective-permute-start(bf16[150,1536]{1,0:T(8,128)(2,1)} %pad_maximum_fusion.1), channel_id=1, source_target_pairs={{0,2},{2,4},{4,6},{6,8},{8,10},{10,12},{12,14},{14,0},{1,3},{3,5},... | collective-permute-start | bytes 1382408 | tf_op jit(solution)/shard_map/ppermute | solution.py:18
  32.8 112.6 %collective-permute-start.3 = (bf16[150,1536]{1,0:T(8,128)(2,1)}, bf16[150,1536]{1,0:T(8,128)(2,1)}, u32[]{:S(2)}, u32[]{:S(2)}) collective-permute-start(bf16[150,1536]{1,0:T(8,128)(2,1)} %pad_maximum_fusion.1), channel_id=1, source_target_pairs={{0,14},{2,0},{4,2},{6,4},{8,6},{10,8},{12,10},{14,12},{1,15},{3,1}... | collective-permute-start | bytes 1382408 | tf_op jit(solution)/shard_map/ppermute | solution.py:18
  36.0 109.4 %collective-permute-start.4 = (bf16[150,1536]{1,0:T(8,128)(2,1)}, bf16[150,1536]{1,0:T(8,128)(2,1)}, u32[]{:S(2)}, u32[]{:S(2)}) collective-permute-start(bf16[150,1536]{1,0:T(8,128)(2,1)} %pad_maximum_fusion.1), channel_id=1, source_target_pairs={{0,12},{2,14},{4,0},{6,2},{8,4},{10,6},{12,8},{14,10},{1,13},{3,15... | collective-permute-start | bytes 1382408 | tf_op jit(solution)/shard_map/ppermute | solution.py:18
  141.2 20.3 %collective-permute-start.5 = (bf16[150,1536]{1,0:T(8,128)(2,1)}, bf16[150,1536]{1,0:T(8,128)(2,1)S(1)}, u32[]{:S(2)}, u32[]{:S(2)}) collective-permute-start(bf16[150,1536]{1,0:T(8,128)(2,1)} %pad_maximum_fusion.1), channel_id=1, source_target_pairs={{0,10},{2,12},{4,14},{6,0},{8,2},{10,4},{12,6},{14,8},{1,11},{3,13... | collective-permute-start | bytes 1382408 | tf_op jit(solution)/shard_map/ppermute | solution.py:18
  199.6 7.7 %copy-start.1 = (bf16[1606,1536]{1,0:T(8,128)(2,1)S(1)}, bf16[1606,1536]{1,0:T(8,128)(2,1)}, u32[]{:S(2)}) copy-start(bf16[1606,1536]{1,0:T(8,128)(2,1)} %concatenate.39) | copy-start | bytes 14800900
Sparse Core Ops, SparseCore 0:
  11.1 126.9 all-reduce.1
  140.1 92.4 all-gather.1
  237.0 8.6 reduce-scatter.1
where the time goes:
time: 254 us; the launch traced here: 252 us
  waiting for transfers between devices  140 us (55%)
  local copies, waits for them, and re-layouts  44.1 us (17%)
  between operations  22.3 us (9%)
  matrix products  19.3 us (8%)
  starting transfers between devices  13.8 us (5%)
  other arithmetic  12.8 us (5%)
    psum x1, waiting for transfers between devices, body(): summed_text = lax.psum(partial_text, 'space')  91.5 us
    concatenate x1, local copies, waits for them, and re-layouts, body(): keys_all = jnp.concatenate(blocks, axis=0)  34.4 us
    all_gather x1, waiting for transfers between devices, body(): lax.all_gather(out_weight, 'space', axis=1, tiled=True)  22.8 us
    ppermute x6, waiting for transfers between devices, shifted(): return lax.ppermute(value, axis, pairs)  16.1 us
    ppermute x6, starting transfers between devices, shifted(): return lax.ppermute(value, axis, pairs)  13.7 us
    dot_general x6, matrix products, body(): lax.dot_general(query_slice, key_slice, (((1,), (1,)), ((), ())), preferr...  9.63 us
    reduce_scatter x1, waiting for transfers between devices, body(): lax.psum_scatter(partial_out.astype(jnp.bfloat16), 'heads', scatter_dimen...  8.8 us
  transfers between devices with their start and end apart: 9, of which 4 were waited for; matrix products, arithmetic and copies ran while one was open for 27% of the time, Pallas kernels for 0%

commit v1 on v0

--- a/solution.py
+++ b/solution.py
@@ -10,6 +10,24 @@
 rope_theta = 256.0
 eps_norm = 1e-06
 masked_score = -1e30
+
+
+def ring_gather(value, axis, dim):
+    ways, here, step = (lax.axis_size(axis), lax.axis_index(axis), value.shape[dim])
+    lengths = [n * ways if d == dim else n for d, n in enumerate(value.shape)]
+    full = lax.dynamic_update_slice_in_dim(
+        jnp.zeros(lengths, value.dtype), value, here * step, axis=dim
+    )
+    going_up = going_down = value
+    for far in range(1, ways // 2 + 1):
+        going_up = lax.ppermute(going_up, axis, [(d, (d + 1) % ways) for d in range(ways)])
+        full = lax.dynamic_update_slice_in_dim(full, going_up, (here - far) % ways * step, axis=dim)
+        if 2 * far < ways:
+            going_down = lax.ppermute(going_down, axis, [(d, (d - 1) % ways) for d in range(ways)])
+            full = lax.dynamic_update_slice_in_dim(
+                full, going_down, (here + far) % ways * step, axis=dim
+            )
+    return full
 
 
 def shifted(value, axis, steps):
@@ -138,9 +156,7 @@
         )
     attended = jnp.concatenate(head_outputs, axis=1)
     partial_out = jnp.dot(
-        attended,
-        lax.all_gather(out_weight, "space", axis=1, tiled=True),
-        preferred_element_type=jnp.float32,
+        attended, ring_gather(out_weight, "space", 1), preferred_element_type=jnp.float32
     )
     summed_out = lax.psum_scatter(
         partial_out.astype(jnp.bfloat16), "heads", scatter_dimension=1, tiled=True

time: 254 us -> 287 us (1.13)
  starting transfers between devices: 13.8 us -> 41.8 us
  local copies, waits for them, and re-layouts: 44.1 us -> 58.2 us
  waiting for transfers between devices: 140 us -> 132 us
    ppermute x0 -> x7, waiting for transfers between devices: none -> 64.7 us  [the longest x4 50.4 us: ring_gather(): lax.ppermute(going_up, axis, [(d, (d + 1) % ways) for d in range(ways)])]
    psum x1, waiting for transfers between devices: 91.5 us -> 54.7 us  [body(): summed_text = lax.psum(partial_text, 'space')]
    ppermute x0 -> x7, starting transfers between devices: none -> 29.9 us  [the longest x4 19.1 us: ring_gather(): lax.ppermute(going_up, axis, [(d, (d + 1) % ways) for d in range(ways)])]
    all_gather x1 -> x0, waiting for transfers between devices: 22.8 us -> none  [body(): lax.all_gather(out_weight, 'space', axis=1, tiled=True)]
    dynamic_update_slice x0 -> x8, local copies, waits for them, and re-layouts: none -> 10.9 us  [the longest x3 5.03 us: ring_gather(): lax.dynamic_update_slice_in_dim(full, going_down, (here + far) % ways * s...]
    ppermute x6, waiting for transfers between devices: 16.1 us -> 5.42 us  [shifted(): return lax.ppermute(value, axis, pairs)]
  transfers between devices with their start and end apart: 9 -> 15, of which waited for: 4 -> 7; matrix products, arithmetic and copies ran while one was open for 27% -> 29% of each run, Pallas kernels for 0% -> 0%
where the time goes in v1:
time: 287 us; the launch traced here: 285 us
  waiting for transfers between devices  132 us (46%)
  local copies, waits for them, and re-layouts  58.2 us (20%)
  starting transfers between devices  41.8 us (15%)
  between operations  22.8 us (8%)
  matrix products  17.1 us (6%)
  other arithmetic  13.4 us (5%)
    psum x1, waiting for transfers between devices, body(): summed_text = lax.psum(partial_text, 'space')  54.7 us
    ppermute x4, waiting for transfers between devices, ring_gather(): lax.ppermute(going_up, axis, [(d, (d + 1) % ways) for d in range(ways)])  50.4 us
    concatenate x1, local copies, waits for them, and re-layouts, body(): keys_all = jnp.concatenate(blocks, axis=0)  36.1 us
    ppermute x4, starting transfers between devices, ring_gather(): lax.ppermute(going_up, axis, [(d, (d + 1) % ways) for d in range(ways)])  19.1 us
    ppermute x3, waiting for transfers between devices, ring_gather(): lax.ppermute(going_down, axis, [(d, (d - 1) % ways) for d in range(ways)])  14.3 us
    ppermute x6, starting transfers between devices, shifted(): return lax.ppermute(value, axis, pairs)  11.8 us
    ppermute x3, starting transfers between devices, ring_gather(): lax.ppermute(going_down, axis, [(d, (d - 1) % ways) for d in range(ways)])  10.8 us
    dot_general x6, matrix products, body(): lax.dot_general(query_slice, key_slice, (((1,), (1,)), ((), ())), preferr...  7.38 us
  transfers between devices with their start and end apart: 15, of which 7 were waited for; matrix products, arithmetic and copies ran while one was open for 29% of the time, Pallas kernels for 0%

profile of v1, /device:TPU:0, one launch (start us, length us, event | category | flops | bytes accessed | tf_op | source)
XLA Modules:
  0.0 285.3 jit_solution(8143537618062802308)
XLA Ops:
  6.5 2.9 %collective-permute-start.6 = (bf16[768,384]{1,0:T(8,128)(2,1)}, bf16[768,384]{1,0:T(8,128)(2,1)}, u32[]{:S(2)}, u32[]{:S(2)}) collective-permute-start(bf16[768,384]{1,0:T(8,128)(2,1)} %param.14), channel_id=1, source_target_pairs={{0,2},{2,4},{4,6},{6,8},{8,10},{10,12},{12,14},{14,0},{1,3},{3,5},... | collective-permute-start | bytes 1769480 | tf_op jit(solution)/shard_map/ppermute | solution.py:23
  9.5 3.1 %collective-permute-start.7 = (bf16[768,384]{1,0:T(8,128)(2,1)}, bf16[768,384]{1,0:T(8,128)(2,1)}, u32[]{:S(2)}, u32[]{:S(2)}) collective-permute-start(bf16[768,384]{1,0:T(8,128)(2,1)} %param.14), channel_id=1, source_target_pairs={{0,14},{2,0},{4,2},{6,4},{8,6},{10,8},{12,10},{14,12},{1,15},{3,1}... | collective-permute-start | bytes 1769480 | tf_op jit(solution)/shard_map/ppermute | solution.py:26
  12.6 3.0 %fusion.6 = f32[256,1536]{1,0:T(8,128)} fusion(bf16[384,768]{1,0:T(8,128)(2,1)} %param.13, bf16[384,768]{1,0:T(8,128)(2,1)} %param.12, bf16[256,3072]{1,0:T(8,128)(2,1)S(1)} %copy-done, s32[]{:T(128)S(6)} %select_n.160), kind=kOutput, calls=%fused_computation.13 | convolution fusion | flops 304349184 | bytes 2949124 | tf_op jit(solution)/shard_map/dot_general | solution.py:116
  15.6 1.3 fusion.52
  19.8 0.5 reshape.201
  20.3 2.0 copy.10
  22.3 1.6 reshape.202
  24.3 2.7 subtract_convert_fusion.1
  27.0 1.0 pad_maximum_fusion.3
  28.0 0.4 convert_element_type.111
  28.5 1.7 pad_maximum_fusion.1
  30.3 1.5 collective-permute-start.1
  31.8 2.4 collective-permute-start.2
  34.2 0.6 fusion.54
  41.2 2.0 pad_maximum_fusion.2
  43.2 0.4 convert_element_type.110
  43.9 6.9 %collective-permute-done.6 = bf16[768,384]{1,0:T(8,128)(2,1)} collective-permute-done((bf16[768,384]{1,0:T(8,128)(2,1)}, bf16[768,384]{1,0:T(8,128)(2,1)}, u32[]{:S(2)}, u32[]{:S(2)}) %collective-permute-start.6) | collective-permute-done | bytes 589856 | tf_op jit(solution)/shard_map/ppermute | solution.py:23
  50.8 2.9 %collective-permute-start.8 = (bf16[768,384]{1,0:T(8,128)(2,1)}, bf16[768,384]{1,0:T(8,128)(2,1)S(1)}, u32[]{:S(2)}, u32[]{:S(2)}) collective-permute-start(bf16[768,384]{1,0:T(8,128)(2,1)} %collective-permute-done.6), channel_id=1, source_target_pairs={{0,2},{2,4},{4,6},{6,8},{8,10},{10,12},{12,14},{14,0},{1,3},{3,5},... | collective-permute-start | bytes 1769480 | tf_op jit(solution)/shard_map/ppermute | solution.py:23
  53.7 2.8 broadcast_in_dim.75
  56.4 1.0 constant_dynamic-update-slice_fusion.7
  57.4 3.6 %collective-permute-start.9 = (bf16[768,384]{1,0:T(8,128)(2,1)}, bf16[768,384]{1,0:T(8,128)(2,1)S(1)}, u32[]{:S(2)}, u32[]{:S(2)}) collective-permute-start(bf16[768,384]{1,0:T(8,128)(2,1)} %collective-permute-done.7), channel_id=1, source_target_pairs={{0,14},{2,0},{4,2},{6,4},{8,6},{10,8},{12,10},{14,12},{1,15},{3,1}... | collective-permute-start | bytes 1769480 | tf_op jit(solution)/shard_map/ppermute | solution.py:26
  61.0 2.0 constant_dynamic-update-slice_fusion.6
  63.0 2.1 constant_dynamic-update-slice_fusion.5
  65.0 21.2 %collective-permute-done.8 = bf16[768,384]{1,0:T(8,128)(2,1)S(1)} collective-permute-done((bf16[768,384]{1,0:T(8,128)(2,1)}, bf16[768,384]{1,0:T(8,128)(2,1)S(1)}, u32[]{:S(2)}, u32[]{:S(2)}) %collective-permute-start.8) | collective-permute-done | bytes 589856 | tf_op jit(solution)/shard_map/ppermute | solution.py:23
  86.3 5.1 %collective-permute-start.3 = (bf16[150,1536]{1,0:T(8,128)(2,1)}, bf16[150,1536]{1,0:T(8,128)(2,1)}, u32[]{:S(2)}, u32[]{:S(2)}) collective-permute-start(bf16[150,1536]{1,0:T(8,128)(2,1)} %pad_maximum_fusion.1), channel_id=1, source_target_pairs={{0,14},{2,0},{4,2},{6,4},{8,6},{10,8},{12,10},{14,12},{1,15},{3,1}... | collective-permute-start | bytes 1382408 | tf_op jit(solution)/shard_map/ppermute | solution.py:36
  91.3 1.0 constant_dynamic-update-slice_fusion.4
  92.4 14.3 %collective-permute-done.9 = bf16[768,384]{1,0:T(8,128)(2,1)S(1)} collective-permute-done((bf16[768,384]{1,0:T(8,128)(2,1)}, bf16[768,384]{1,0:T(8,128)(2,1)S(1)}, u32[]{:S(2)}, u32[]{:S(2)}) %collective-permute-start.9) | collective-permute-done | bytes 589856 | tf_op jit(solution)/shard_map/ppermute | solution.py:26
  106.6 0.8 copy-done.3
  107.5 0.9 constant_dynamic-update-slice_fusion.3
  108.4 54.7 %all-reduce.2.cloned.1.call-done = f32[256,1536]{1,0:T(8,128)} async-done(((f32[256,1536]{1,0:T(8,128)}), f32[256,1536]{1,0:T(8,128)}) %all-reduce.2.cloned.1.call-update) | async-done | bytes 1572880 | tf_op jit(solution)/shard_map/psum | solution.py:117
  163.1 1.2 slice_multiply_fusion
  164.3 0.3 copy.12
  165.0 1.2 slice.180
  166.2 2.8 collective-permute-start.5
  168.9 1.2 multiply_convert_fusion
  170.2 0.6 collective-permute-start.10
  170.8 4.2 %collective-permute-start.11 = (bf16[768,384]{1,0:T(8,128)(2,1)}, bf16[768,384]{1,0:T(8,128)(2,1)}, u32[]{:S(2)}, u32[]{:S(2)}) collective-permute-start(bf16[768,384]{1,0:T(8,128)(2,1)} %copy-done.3), channel_id=1, source_target_pairs={{0,14},{2,0},{4,2},{6,4},{8,6},{10,8},{12,10},{14,12},{1,15},{3,1}... | collective-permute-start | bytes 1769480 | tf_op jit(solution)/shard_map/ppermute | solution.py:26
  175.0 5.4 %collective-permute-done.5 = bf16[150,1536]{1,0:T(8,128)(2,1)} collective-permute-done((bf16[150,1536]{1,0:T(8,128)(2,1)}, bf16[150,1536]{1,0:T(8,128)(2,1)}, u32[]{:S(2)}, u32[]{:S(2)}) %collective-permute-start.5) | collective-permute-done | bytes 460832 | tf_op jit(solution)/shard_map/ppermute | solution.py:36
  180.4 36.1 %concatenate.39 = bf16[1606,1536]{1,0:T(8,128)(2,1)} concatenate(bf16[150,1536]{1,0:T(8,128)(2,1)} %collective-permute-done, bf16[150,1536]{1,0:T(8,128)(2,1)} %collective-permute-done.1, bf16[150,1536]{1,0:T(8,128)(2,1)} %collective-permute-done.2, bf16[150,1536]{1,0:T(8,128)(2,1)} %collective-permute-done.2, bf16[150,1536]{1,0:T(8,128)(2,1)} %pad_maximum_fusion.1, ...), dimensions={0} | concatenate | bytes 9867264 | tf_op jit(solution)/shard_map/concatenate | solution.py:135
  216.5 1.7 fusion.55
  218.2 1.5 fusion.56
  219.8 1.5 fusion.57
  221.3 1.5 fusion.58
  222.8 0.5 fusion.59
  223.4 0.3 fusion.16
  223.7 0.4 fusion.15
  224.1 0.3 fusion.17
  224.4 0.4 fusion.14
  224.8 0.3 fusion.18
  225.1 0.4 fusion.13
  225.5 0.3 fusion.19
  225.8 0.4 fusion.12
  226.2 0.3 fusion.20
  226.5 0.4 fusion.11
  227.0 0.5 fusion.60
  227.5 12.6 %collective-permute-start.12 = (bf16[768,384]{1,0:T(8,128)(2,1)S(1)}, bf16[768,384]{1,0:T(8,128)(2,1)S(1)}, u32[]{:S(2)}, u32[]{:S(2)}) collective-permute-start(bf16[768,384]{1,0:T(8,128)(2,1)S(1)} %collective-permute-done.10), channel_id=1, source_target_pairs={{0,2},{2,4},{4,6},{6,8},{8,10},{10,12},{12,14},{14,0},{1,3},{3,5},... | collective-permute-start | bytes 1769480 | tf_op jit(solution)/shard_map/ppermute | solution.py:23
  240.2 0.3 fusion.21
  240.4 0.4 fusion.10
  240.9 1.0 constant_dynamic-update-slice_fusion.2
  241.8 2.0 constant_dynamic-update-slice_fusion.1
  243.9 22.3 %collective-permute-done.12 = bf16[768,384]{1,0:T(8,128)(2,1)S(1)} collective-permute-done((bf16[768,384]{1,0:T(8,128)(2,1)S(1)}, bf16[768,384]{1,0:T(8,128)(2,1)S(1)}, u32[]{:S(2)}, u32[]{:S(2)}) %collective-permute-start.12) | collective-permute-done | bytes 589856 | tf_op jit(solution)/shard_map/ppermute | solution.py:23
  266.2 0.9 constant_dynamic-update-slice_fusion
  267.2 4.2 %convolution_convert_fusion = bf16[150,3072]{1,0:T(8,128)(2,1)} fusion(bf16[150,768]{1,0:T(8,128)(2,1)S(1)} %fusion.10, bf16[768,3072]{1,0:T(8,128)(2,1)} %constant_dynamic-update-slice_fusion), kind=kOutput, calls=%fused_computation | convolution fusion | flops 708249600 | bytes 5870592 | tf_op jit(solution)/shard_map/dot_general | solution.py:158
  271.4 7.1 %reduce-scatter.2.cloned.1.call-done = bf16[150,1536]{1,0:T(8,128)(2,1)} async-done(((bf16[150,3072]{1,0:T(8,128)(2,1)}), bf16[150,1536]{1,0:T(8,128)(2,1)}) %reduce-scatter.2.cloned.1.call-update) | async-done | bytes 460816 | tf_op jit(solution)/shard_map/reduce_scatter | solution.py:161
  (53 shorter events, 1.5 us)
Async XLA Ops:
  6.5 6.1 %copy-start = (bf16[256,3072]{1,0:T(8,128)(2,1)S(1)}, bf16[256,3072]{1,0:T(8,128)(2,1)}, u32[]{:S(2)}) copy-start(bf16[256,3072]{1,0:T(8,128)(2,1)} %param.11) | copy-start | bytes 4718596
  6.5 13.0 %copy-start.5 = (bf16[150,768]{1,0:T(8,128)(2,1)S(1)}, bf16[150,768]{1,0:T(8,128)(2,1)}, u32[]{:S(2)}) copy-start(bf16[150,768]{1,0:T(8,128)(2,1)} %param.8) | copy-start | bytes 691204
  6.5 156.6 %all-reduce.2.cloned.1.call-start = ((), (), s32[]{:S(2)}) async-start(), calls=%async_computation.1 | async-start | bytes 3145728 | tf_op jit(solution)/shard_map/psum | solution.py:117
  6.5 44.2 %collective-permute-start.6 = (bf16[768,384]{1,0:T(8,128)(2,1)}, bf16[768,384]{1,0:T(8,128)(2,1)}, u32[]{:S(2)}, u32[]{:S(2)}) collective-permute-start(bf16[768,384]{1,0:T(8,128)(2,1)} %param.14), channel_id=1, source_target_pairs={{0,2},{2,4},{4,6},{6,8},{8,10},{10,12},{12,14},{14,0},{1,3},{3,5},... | collective-permute-start | bytes 1769480 | tf_op jit(solution)/shard_map/ppermute | solution.py:23
  9.5 48.0 %collective-permute-start.7 = (bf16[768,384]{1,0:T(8,128)(2,1)}, bf16[768,384]{1,0:T(8,128)(2,1)}, u32[]{:S(2)}, u32[]{:S(2)}) collective-permute-start(bf16[768,384]{1,0:T(8,128)(2,1)} %param.14), channel_id=1, source_target_pairs={{0,14},{2,0},{4,2},{6,4},{8,6},{10,8},{12,10},{14,12},{1,15},{3,1}... | collective-permute-start | bytes 1769480 | tf_op jit(solution)/shard_map/ppermute | solution.py:26
  15.6 262.8 %reduce-scatter.2.cloned.1.call-start = ((), (), s32[]{:S(2)}) async-start(), calls=%async_computation.2 | async-start | bytes 1400832 | tf_op jit(solution)/shard_map/reduce_scatter | solution.py:161
  20.3 14.0 %copy-start.6 = (s32[8]{0:T(128)S(1)}, s32[8]{0:T(128)}, u32[]{:S(2)}) copy-start(s32[8]{0:T(128)} %param.15) | copy-start | bytes 100
  28.0 28.4 %copy-start.2 = (bf16[768,384]{1,0:T(8,128)(2,1)S(1)}, bf16[768,384]{1,0:T(8,128)(2,1)}, u32[]{:S(2)}) copy-start(bf16[768,384]{1,0:T(8,128)(2,1)} %param.14) | copy-start | bytes 1769476
  30.3 135.9 %collective-permute-start = (bf16[150,1536]{1,0:T(8,128)(2,1)}, bf16[150,1536]{1,0:T(8,128)(2,1)}, u32[]{:S(2)}, u32[]{:S(2)}) collective-permute-start(bf16[150,1536]{1,0:T(8,128)(2,1)} %pad_maximum_fusion.1), channel_id=1, source_target_pairs={{0,6},{2,8},{4,10},{6,12},{8,14},{10,0},{12,2},{14,4},{1,7},{3,9},... | collective-permute-start | bytes 1382408 | tf_op jit(solution)/shard_map/ppermute | solution.py:36
  30.3 139.9 %collective-permute-start.1 = (bf16[150,1536]{1,0:T(8,128)(2,1)}, bf16[150,1536]{1,0:T(8,128)(2,1)}, u32[]{:S(2)}, u32[]{:S(2)}) collective-permute-start(bf16[150,1536]{1,0:T(8,128)(2,1)} %pad_maximum_fusion.1), channel_id=1, source_target_pairs={{0,4},{2,6},{4,8},{6,10},{8,12},{10,14},{12,0},{14,2},{1,5},{3,7},... | collective-permute-start | bytes 1382408 | tf_op jit(solution)/shard_map/ppermute | solution.py:36
  31.8 139.0 %collective-permute-start.2 = (bf16[150,1536]{1,0:T(8,128)(2,1)}, bf16[150,1536]{1,0:T(8,128)(2,1)}, u32[]{:S(2)}, u32[]{:S(2)}) collective-permute-start(bf16[150,1536]{1,0:T(8,128)(2,1)} %pad_maximum_fusion.1), channel_id=1, source_target_pairs={{0,2},{2,4},{4,6},{6,8},{8,10},{10,12},{12,14},{14,0},{1,3},{3,5},... | collective-permute-start | bytes 1382408 | tf_op jit(solution)/shard_map/ppermute | solution.py:36
  50.8 35.5 %collective-permute-start.8 = (bf16[768,384]{1,0:T(8,128)(2,1)}, bf16[768,384]{1,0:T(8,128)(2,1)S(1)}, u32[]{:S(2)}, u32[]{:S(2)}) collective-permute-start(bf16[768,384]{1,0:T(8,128)(2,1)} %collective-permute-done.6), channel_id=1, source_target_pairs={{0,2},{2,4},{4,6},{6,8},{8,10},{10,12},{12,14},{14,0},{1,3},{3,5},... | collective-permute-start | bytes 1769480 | tf_op jit(solution)/shard_map/ppermute | solution.py:23
  57.4 49.2 %collective-permute-start.9 = (bf16[768,384]{1,0:T(8,128)(2,1)}, bf16[768,384]{1,0:T(8,128)(2,1)S(1)}, u32[]{:S(2)}, u32[]{:S(2)}) collective-permute-start(bf16[768,384]{1,0:T(8,128)(2,1)} %collective-permute-done.7), channel_id=1, source_target_pairs={{0,14},{2,0},{4,2},{6,4},{8,6},{10,8},{12,10},{14,12},{1,15},{3,1}... | collective-permute-start | bytes 1769480 | tf_op jit(solution)/shard_map/ppermute | solution.py:26
  86.3 20.4 %copy-start.4 = (bf16[768,384]{1,0:T(8,128)(2,1)}, bf16[768,384]{1,0:T(8,128)(2,1)S(1)}, u32[]{:S(2)}) copy-start(bf16[768,384]{1,0:T(8,128)(2,1)S(1)} %collective-permute-done.8) | copy-start | bytes 1769476
  86.3 88.7 %collective-permute-start.3 = (bf16[150,1536]{1,0:T(8,128)(2,1)}, bf16[150,1536]{1,0:T(8,128)(2,1)}, u32[]{:S(2)}, u32[]{:S(2)}) collective-permute-start(bf16[150,1536]{1,0:T(8,128)(2,1)} %pad_maximum_fusion.1), channel_id=1, source_target_pairs={{0,14},{2,0},{4,2},{6,4},{8,6},{10,8},{12,10},{14,12},{1,15},{3,1}... | collective-permute-start | bytes 1382408 | tf_op jit(solution)/shard_map/ppermute | solution.py:36
  106.6 0.8 copy-start.3
  106.6 68.4 %collective-permute-start.4 = (bf16[150,1536]{1,0:T(8,128)(2,1)}, bf16[150,1536]{1,0:T(8,128)(2,1)}, u32[]{:S(2)}, u32[]{:S(2)}) collective-permute-start(bf16[150,1536]{1,0:T(8,128)(2,1)} %pad_maximum_fusion.1), channel_id=1, source_target_pairs={{0,12},{2,14},{4,0},{6,2},{8,4},{10,6},{12,8},{14,10},{1,13},{3,15... | collective-permute-start | bytes 1382408 | tf_op jit(solution)/shard_map/ppermute | solution.py:36
  166.2 14.2 %collective-permute-start.5 = (bf16[150,1536]{1,0:T(8,128)(2,1)}, bf16[150,1536]{1,0:T(8,128)(2,1)}, u32[]{:S(2)}, u32[]{:S(2)}) collective-permute-start(bf16[150,1536]{1,0:T(8,128)(2,1)} %pad_maximum_fusion.1), channel_id=1, source_target_pairs={{0,10},{2,12},{4,14},{6,0},{8,2},{10,4},{12,6},{14,8},{1,11},{3,13... | collective-permute-start | bytes 1382408 | tf_op jit(solution)/shard_map/ppermute | solution.py:36
  170.2 57.3 %collective-permute-start.10 = (bf16[768,384]{1,0:T(8,128)(2,1)}, bf16[768,384]{1,0:T(8,128)(2,1)S(1)}, u32[]{:S(2)}, u32[]{:S(2)}) collective-permute-start(bf16[768,384]{1,0:T(8,128)(2,1)} %copy-done.4), channel_id=1, source_target_pairs={{0,2},{2,4},{4,6},{6,8},{8,10},{10,12},{12,14},{14,0},{1,3},{3,5},... | collective-permute-start | bytes 1769480 | tf_op jit(solution)/shard_map/ppermute | solution.py:23
  170.8 71.0 %collective-permute-start.11 = (bf16[768,384]{1,0:T(8,128)(2,1)}, bf16[768,384]{1,0:T(8,128)(2,1)}, u32[]{:S(2)}, u32[]{:S(2)}) collective-permute-start(bf16[768,384]{1,0:T(8,128)(2,1)} %copy-done.3), channel_id=1, source_target_pairs={{0,14},{2,0},{4,2},{6,4},{8,6},{10,8},{12,10},{14,12},{1,15},{3,1}... | collective-permute-start | bytes 1769480 | tf_op jit(solution)/shard_map/ppermute | solution.py:26
  216.5 6.3 %copy-start.1 = (bf16[1606,1536]{1,0:T(8,128)(2,1)S(1)}, bf16[1606,1536]{1,0:T(8,128)(2,1)}, u32[]{:S(2)}) copy-start(bf16[1606,1536]{1,0:T(8,128)(2,1)} %concatenate.39) | copy-start | bytes 14800900
  227.5 38.7 %collective-permute-start.12 = (bf16[768,384]{1,0:T(8,128)(2,1)S(1)}, bf16[768,384]{1,0:T(8,128)(2,1)S(1)}, u32[]{:S(2)}, u32[]{:S(2)}) collective-permute-start(bf16[768,384]{1,0:T(8,128)(2,1)S(1)} %collective-permute-done.10), channel_id=1, source_target_pairs={{0,2},{2,4},{4,6},{6,8},{8,10},{10,12},{12,14},{14,0},{1,3},{3,5},... | collective-permute-start | bytes 1769480 | tf_op jit(solution)/shard_map/ppermute | solution.py:23
Sparse Core Ops, SparseCore 0:
  15.7 147.3 all-reduce.1
  271.5 6.8 reduce-scatter.1
